TPU v7x, 512 devices: a whole 4x8x8 slice. The times are simulated.
512 devices in a mesh: ctx: 32 (over x, y), tp: 16 (over z, core).
Axes of the slice: x: 4, y: 8, z: 8, core: 2. Of those that a mesh axis runs over, the one named last changes fastest.
Arguments:
- prefix_x: bfloat16 [8192, 8192], P('ctx', 'tp'), may hold values from -6 to 6
- prefix_z: bfloat16 [8192, 8192], P('ctx', 'tp'), may hold values from -6 to 6
- prefix_bc: bfloat16 [8192, 256], P(('ctx', 'tp')), may hold values from -6 to 6
- prefix_dt: float32 [128, 8192], P('tp', 'ctx'), may hold values from -6 to 6
- branch_x: bfloat16 [8192, 8192], P('ctx', 'tp'), may hold values from -6 to 6
- branch_z: bfloat16 [8192, 8192], P('ctx', 'tp'), may hold values from -6 to 6
- branch_bc: bfloat16 [8192, 256], P(('ctx', 'tp')), may hold values from -6 to 6
- branch_dt: float32 [128, 8192], P('tp', 'ctx'), may hold values from -6 to 6
- conv_x: bfloat16 [4, 8192], P(None, 'tp'), may hold values from -3 to 3
- conv_bc: bfloat16 [4, 256], replicated, may hold values from -3 to 3
- decay_rate: float32 [128], P('tp'), may hold values from 2.4414063e-05 to 0.03
- skip: float32 [128], P('tp'), may hold values from 0.5 to 1.5
- norm_gain: float32 [8192], P('tp'), may hold values from 0.5 to 1.5
- bound_pos: int32 [8], replicated, may hold values from 0 to 8191
- branch_owner: int32 [64], replicated, may hold values from 0 to 31, as said below
- branch_parent: int32 [64], replicated, may hold values from 0 to 7
- branch_len: int32 [64], replicated, may hold values from 1 to 255, as said below
Outputs:
- prefix_out: bfloat16 [8192, 8192], P('ctx', 'tp')
- branch_out: bfloat16 [8192, 8192], P('ctx', 'tp')
Inputs may be any that keep to these rules, and one draw needn't show every extreme that they name: `branch_owner`: every block index 0 to 31 holds exactly 2 branches. `branch_len`: the branches of one block have lengths that sum to at most 256; in every draw some block's sum is exactly 256, and some branch has exactly 255 rows.
All inputs are finite; a program needn't handle non-finite values.
Results may differ from a plain program's by a relative error of at most 0.0034.
Values may be sent and summed in bfloat16 or wider, within the bound.
No kernel may reach another device: no remote copies, remote signals or barrier semaphores. Data moves between devices by JAX's collectives and lax.ppermute only.
A program may use at most 64 MiB of HBM per device.

v0:
```python
import jax
import jax.numpy as jnp
from jax import lax
from jax.sharding import PartitionSpec as P

NORM_GROUP = 8192
BR_PER = 2
EPSILON = 1e-05


def passed_along(value, axis, steps):
    count = lax.axis_size(axis)
    first, last = (max(0, -steps), min(count, count - steps))
    return lax.ppermute(value, axis, [(source, source + steps) for source in range(first, last)])


def conv_silu(lagged, weights):
    summed = weights[0].astype(jnp.float32)[None, :] * lagged[0].astype(jnp.float32)
    for tap_index in range(1, len(lagged)):
        summed = summed + weights[tap_index].astype(jnp.float32)[None, :] * lagged[
            tap_index
        ].astype(jnp.float32)
    return jax.nn.silu(summed).astype(jnp.bfloat16)


def split_conv(convolved, channels, head_count):
    length = convolved.shape[0]
    state_size = (convolved.shape[1] - channels) // 2
    values = convolved[:, :channels].reshape(length, head_count, channels // head_count)
    return (
        values,
        convolved[:, channels : channels + state_size],
        convolved[:, channels + state_size :],
    )


def decays(raw_steps, rates):
    step_size = jax.nn.softplus(raw_steps)
    log_decay = -rates[:, None] * step_size
    return (step_size, log_decay, jnp.cumsum(log_decay, axis=1))


def intra_block(values, b_rows, c_rows, step_size, cumulative, causal_mask):
    scores = jnp.dot(c_rows, b_rows.T, preferred_element_type=jnp.float32)
    exponent = jnp.where(causal_mask[None], cumulative[:, :, None] - cumulative[:, None, :], 0.0)
    mixing = jnp.where(
        causal_mask[None], scores[None] * jnp.exp(exponent) * step_size[:, None, :], 0.0
    ).astype(jnp.bfloat16)
    return jnp.einsum("hts,shp->thp", mixing, values, preferred_element_type=jnp.float32)


def local_states(values, b_rows, step_size, cumulative, positions):
    length = cumulative.shape[1]
    clipped = jnp.clip(positions, 0, length - 1)
    decay_end = jnp.take(cumulative, clipped, axis=1)
    row_index = jnp.arange(length, dtype=jnp.int32)
    inside = row_index[None, :] <= positions[:, None]
    exponent = jnp.where(inside[:, None, :], decay_end.T[:, :, None] - cumulative[None], 0.0)
    weight = jnp.where(inside[:, None, :], jnp.exp(exponent) * step_size[None], 0.0)
    weighted = (
        jnp.transpose(weight, (0, 2, 1))[:, :, :, None] * values[None].astype(jnp.float32)
    ).astype(jnp.bfloat16)
    return jnp.einsum("jshp,sn->jhpn", weighted, b_rows, preferred_element_type=jnp.float32)


def from_state(c_rows, state, weight):
    result = jnp.einsum(
        "tn,hpn->thp", c_rows.astype(jnp.float32), state, precision=lax.Precision.HIGHEST
    )
    return result * weight.T[:, :, None]


def finish(mixed_out, values, skip, gate_rows, gain):
    length = mixed_out.shape[0]
    mixed_out = mixed_out + skip[None, :, None] * values.astype(jnp.float32)
    gated = mixed_out.reshape(length, -1) * jax.nn.silu(gate_rows.astype(jnp.float32))
    partial_squares = jnp.sum(gated * gated, axis=1, keepdims=True)
    total_squares = lax.psum(partial_squares, "tp")
    factor = lax.rsqrt(total_squares / NORM_GROUP + EPSILON)
    return (gated * factor * gain[None, :]).astype(jnp.bfloat16)


def layout(owner_index, branch_owner, branch_parent, branch_len, length):
    owned = (branch_owner == owner_index).astype(jnp.int32)
    owned_rank = jnp.cumsum(owned) - 1
    owned_lengths = owned * branch_len
    starts = jnp.cumsum(owned_lengths) - owned_lengths
    branch_slot = jnp.arange(BR_PER, dtype=jnp.int32)
    chosen = owned[None, :] * (owned_rank[None, :] == branch_slot[:, None]).astype(jnp.int32)
    segment_length = jnp.sum(chosen * branch_len[None, :], axis=1)
    segment_start = jnp.sum(chosen * starts[None, :], axis=1)
    parents = jnp.sum(chosen * branch_parent[None, :], axis=1)
    row_index = jnp.arange(length, dtype=jnp.int32)
    inside = (
        (row_index[None, :] >= segment_start[:, None])
        & (row_index[None, :] < (segment_start + segment_length)[:, None])
    ).astype(jnp.int32)
    live_count = jnp.sum(inside, axis=0)
    segment = jnp.sum(inside * branch_slot[:, None], axis=0) + BR_PER * (1 - live_count)
    offset = row_index - jnp.sum(inside * segment_start[:, None], axis=0)
    return (segment, offset, live_count > 0, parents)


def branch_block(
    joined_rows,
    gate_rows,
    raw_steps,
    all_states,
    all_tails,
    weights,
    rates,
    skip,
    gain,
    owner_index,
    branch_owner,
    branch_parent,
    branch_len,
):
    length, row_width = joined_rows.shape
    channels = gate_rows.shape[1]
    head_count = rates.shape[0]
    tail_count = weights.shape[0] - 1
    segment, offset, live_rows, parents = layout(
        owner_index, branch_owner, branch_parent, branch_len, length
    )
    seed_states = jnp.take(all_states, parents, axis=0)
    tail_rows = jnp.take(all_tails, parents, axis=0).reshape(-1, row_width).astype(jnp.bfloat16)
    column = jnp.arange(tail_rows.shape[0], dtype=jnp.int32)
    column_segment = column // tail_count
    column_row = column % tail_count
    lagged = []
    for tap_index in range(tail_count + 1):
        shift_rows = tail_count - tap_index
        if shift_rows == 0:
            lagged.append(joined_rows)
        else:
            shifted = jnp.concatenate(
                [
                    jnp.zeros((shift_rows, row_width), jnp.bfloat16),
                    joined_rows[: length - shift_rows],
                ],
                axis=0,
            )
            local_rows = jnp.where(
                (offset >= shift_rows)[:, None], shifted, jnp.zeros_like(shifted)
            )
            picker = (
                (segment[:, None] == column_segment[None, :])
                & (offset[:, None] < shift_rows)
                & (column_row[None, :] == tail_count - shift_rows + offset[:, None])
            ).astype(jnp.bfloat16)
            tail_part = jnp.dot(picker, tail_rows, preferred_element_type=jnp.float32).astype(
                jnp.bfloat16
            )
            lagged.append(local_rows + tail_part)
    values, b_rows, c_rows = split_conv(conv_silu(lagged, weights), channels, head_count)
    step_size, log_decay, cumulative = decays(raw_steps, rates)
    row_index = jnp.arange(length, dtype=jnp.int32)
    causal_mask = (
        (segment[:, None] == segment[None, :])
        & live_rows[:, None]
        & (row_index[None, :] <= row_index[:, None])
    )
    mixed_out = intra_block(values, b_rows, c_rows, step_size, cumulative, causal_mask)
    first_rows = jnp.clip(row_index - offset, 0, length - 1)
    start_log = jnp.take(cumulative - log_decay, first_rows, axis=1)
    seed_weight = jnp.where(
        live_rows[None, :], jnp.exp(jnp.where(live_rows[None, :], cumulative - start_log, 0.0)), 0.0
    )
    for branch_slot in range(seed_states.shape[0]):
        portion = from_state(c_rows, seed_states[branch_slot], seed_weight)
        mixed_out = mixed_out + jnp.where((segment == branch_slot)[:, None, None], portion, 0.0)
    result = finish(mixed_out, values, skip, gate_rows, gain)
    return jnp.where(live_rows[:, None], result, jnp.zeros_like(result))


def body(
    prefix_x,
    prefix_z,
    prefix_bc,
    prefix_dt,
    branch_x,
    branch_z,
    branch_bc,
    branch_dt,
    conv_x,
    conv_bc,
    decay_rate,
    skip,
    norm_gain,
    bound_pos,
    branch_owner,
    branch_parent,
    branch_len,
):
    prefix_gathered, branch_gathered = (
        lax.all_gather(prefix_bc, "tp", axis=0, tiled=True),
        lax.all_gather(branch_bc, "tp", axis=0, tiled=True),
    )
    length = prefix_x.shape[0]
    channels = prefix_x.shape[1]
    head_count = decay_rate.shape[0]
    weights = jnp.concatenate([conv_x, conv_bc], axis=1)
    tail_count = weights.shape[0] - 1
    joined_rows = jnp.concatenate([prefix_x, prefix_gathered], axis=1)
    before = passed_along(joined_rows[length - tail_count :], "ctx", 1)
    extended = jnp.concatenate([before, joined_rows], axis=0)
    lagged = [extended[tap_index : tap_index + length] for tap_index in range(tail_count + 1)]
    values, b_rows, c_rows = split_conv(conv_silu(lagged, weights), channels, head_count)
    step_size, log_decay, cumulative = decays(prefix_dt, decay_rate)
    row_index = jnp.arange(length, dtype=jnp.int32)
    causal_mask = row_index[None, :] <= row_index[:, None]
    mixed_out = intra_block(values, b_rows, c_rows, step_size, cumulative, causal_mask)
    owner_index = lax.axis_index("ctx")
    local_at = jnp.where(bound_pos // length == owner_index, bound_pos - owner_index * length, -1)
    positions = jnp.concatenate([local_at, jnp.full((1,), length - 1, jnp.int32)])
    states = local_states(values, b_rows, step_size, cumulative, positions)
    bound_count = bound_pos.shape[0]
    end_state = states[bound_count]
    end_decay = jnp.exp(cumulative[:, -1])

    def carry_step(unused, state):
        return passed_along(end_decay[:, None, None] * state + end_state, "ctx", 1)

    entering = lax.fori_loop(0, lax.axis_size("ctx") - 1, carry_step, jnp.zeros_like(end_state))
    mixed_out = mixed_out + from_state(c_rows, entering, jnp.exp(cumulative))
    prefix_out = finish(mixed_out, values, skip, prefix_z, norm_gain)
    held_here = local_at >= 0
    decay_at = jnp.exp(jnp.take(cumulative, jnp.clip(local_at, 0, length - 1), axis=1))
    candidate = jnp.where(
        held_here[:, None, None, None],
        decay_at.T[:, :, None, None] * entering[None] + states[:bound_count],
        0.0,
    )
    tail_index = (local_at[:, None] + 1 + jnp.arange(tail_count, dtype=jnp.int32)[None, :]).reshape(
        -1
    )
    held_rows = jnp.repeat(held_here, tail_count)
    picker = (
        (jnp.arange(length + tail_count, dtype=jnp.int32)[None, :] == tail_index[:, None])
        & held_rows[:, None]
    ).astype(jnp.bfloat16)
    tail_rows = jnp.dot(picker, extended, preferred_element_type=jnp.float32).reshape(
        bound_count, tail_count, -1
    )
    all_states, all_tails = lax.psum((candidate, tail_rows), "ctx")
    branch_joined = jnp.concatenate([branch_x, branch_gathered], axis=1)
    branch_out = branch_block(
        branch_joined,
        branch_z,
        branch_dt,
        all_states,
        all_tails,
        weights,
        decay_rate,
        skip,
        norm_gain,
        owner_index,
        branch_owner,
        branch_parent,
        branch_len,
    )
    return (prefix_out, branch_out)


def solution(mesh):
    in_specs = (
        P("ctx", "tp"),
        P("ctx", "tp"),
        P(("ctx", "tp"), None),
        P("tp", "ctx"),
        P("ctx", "tp"),
        P("ctx", "tp"),
        P(("ctx", "tp"), None),
        P("tp", "ctx"),
        P(None, "tp"),
        P(),
        P("tp"),
        P("tp"),
        P("tp"),
        P(),
        P(),
        P(),
        P(),
    )
    out_specs = (P("ctx", "tp"), P("ctx", "tp"))
    return jax.shard_map(body, mesh=mesh, in_specs=in_specs, out_specs=out_specs, check_vma=False)
```

profile of v0, /device:TPU:1, one launch (start us, length us, event | category | flops | bytes accessed | tf_op | source)
XLA Modules:
  0.0 639.3 jit_solution(6690966973142288056)
XLA Ops:
  8.3 25.1 %all_gather.6 = bf16[256,256]{1,0:T(8,128)(2,1)S(1)} all-gather(bf16[16,256]{1,0:T(8,128)(2,1)} %param.21), channel_id=1, replica_groups=mesh['ctx'=32,'tp'=16] {'tp'}, dimensions={0}, use_global_device_ids=true | all-gather | bytes 139264 | tf_op jit(solution)/shard_map/all_gather | solution.py:197
  50.8 14.8 %all_gather.7 = bf16[256,256]{1,0:T(8,128)(2,1)S(1)} all-gather(bf16[16,256]{1,0:T(8,128)(2,1)S(1)} %copy-done.27), channel_id=1, replica_groups=mesh['ctx'=32,'tp'=16] {'tp'}, dimensions={0}, use_global_device_ids=true | all-gather | bytes 139264 | tf_op jit(solution)/shard_map/all_gather | solution.py:198
  74.3 305.5 %while.10 = (s32[]{:T(128)}, f32[8,64,128]{2,1,0:T(8,128)S(1)}, f32[8]{0:T(128)}, f32[8,64,128]{2,1,0:T(8,128)S(1)}, s32[]{:T(128)}) while((s32[]{:T(128)}, f32[8,64,128]{2,1,0:T(8,128)S(1)}, f32[8]{0:T(128)}, f32[8,64,128]{2,1,0:T(8,128)S(1)}, s32[]{:T(128)}) %tuple.49), condition=%wide.region_3.4_spmd, body=%wide.region_2.3_spmd.sunk | while | flops 131074 | bytes 1835141 | solution.py:225
  78.2 5.5 collective-permute-done
  84.4 4.1 collective-permute-start
  88.6 4.6 collective-permute-done
  93.9 4.1 collective-permute-start
  98.0 3.7 collective-permute-done
  102.4 4.1 collective-permute-start
  106.5 3.3 collective-permute-done
  110.5 3.8 collective-permute-start
  114.3 3.3 collective-permute-done
  118.3 4.4 collective-permute-start
  122.8 3.3 collective-permute-done
  126.8 5.3 collective-permute-start
  132.1 3.3 collective-permute-done
  136.1 5.0 collective-permute-start
  141.1 3.3 collective-permute-done
  145.1 5.0 collective-permute-start
  150.2 4.0 collective-permute-done
  154.9 5.5 collective-permute-start
  160.3 5.0 collective-permute-done
  166.1 5.9 collective-permute-start
  172.0 6.0 collective-permute-done
  178.7 5.4 collective-permute-start
  184.0 4.8 collective-permute-done
  189.5 5.1 collective-permute-start
  194.6 3.7 collective-permute-done
  199.0 4.2 collective-permute-start
  203.2 3.3 collective-permute-done
  207.2 5.3 collective-permute-start
  216.5 5.3 collective-permute-start
  221.9 3.3 collective-permute-done
  225.8 5.5 collective-permute-start
  235.3 5.0 collective-permute-start
  240.3 3.3 collective-permute-done
  244.3 5.2 collective-permute-start
  249.5 4.2 collective-permute-done
  254.5 5.3 collective-permute-start
  259.8 5.0 collective-permute-done
  265.5 4.3 collective-permute-start
  269.9 5.6 collective-permute-done
  276.2 4.1 collective-permute-start
  280.4 5.7 collective-permute-done
  286.7 5.1 collective-permute-start
  291.9 5.8 collective-permute-done
  298.4 6.9 %collective-permute-start = (f32[8,64,128]{2,1,0:T(8,128)S(1)}, f32[8,64,128]{2,1,0:T(8,128)S(1)}, u32[]{:S(2)}, u32[]{:S(2)}) collective-permute-start(f32[8,64,128]{2,1,0:T(8,128)S(1)} %multiply_add_fusion.4), channel_id=1, source_target_pairs={{0,16},{16,32},{32,48},{48,64},{64,80},{80,96},{96,112},{112,128},... | collective-permute-start | bytes 786440 | tf_op jit(solution)/shard_map/while/body/eval_jaxpr/ppermute | solution.py:14
  305.3 5.0 collective-permute-done
  311.0 6.1 collective-permute-start
  317.2 3.7 collective-permute-done
  321.5 6.8 %collective-permute-start = (f32[8,64,128]{2,1,0:T(8,128)S(1)}, f32[8,64,128]{2,1,0:T(8,128)S(1)}, u32[]{:S(2)}, u32[]{:S(2)}) collective-permute-start(f32[8,64,128]{2,1,0:T(8,128)S(1)} %multiply_add_fusion.4), channel_id=1, source_target_pairs={{0,16},{16,32},{32,48},{48,64},{64,80},{80,96},{96,112},{112,128},... | collective-permute-start | bytes 786440 | tf_op jit(solution)/shard_map/while/body/eval_jaxpr/ppermute | solution.py:14
  328.4 3.3 collective-permute-done
  332.3 5.0 collective-permute-start
  337.3 3.3 collective-permute-done
  341.3 5.3 collective-permute-start
  346.6 3.3 collective-permute-done
  350.6 5.0 collective-permute-start
  355.7 3.3 collective-permute-done
  359.6 6.1 collective-permute-start
  369.7 6.2 collective-permute-start
  375.9 3.8 collective-permute-done
  385.2 129.7 %psum.29 = bf16[8,3,768]{2,1,0:T(4,128)(2,1)S(1)} all-reduce(f32[8,3,768]{2,1,0:T(4,128)S(1)} %reshape.508), channel_id=1, replica_groups=mesh['ctx'=32,'tp'=16] {'ctx'}, use_global_device_ids=true, to_apply=%region_14.15 | all-reduce | flops 18432 | bytes 110592 | tf_op jit(solution)/shard_map/psum | solution.py:246
  520.7 75.1 %all-reduce.6.cloned.1.call-done = f32[8,8,64,128]{3,2,1,0:T(8,128)} async-done(((f32[8,8,64,128]{3,2,1,0:T(8,128)}), f32[8,8,64,128]{3,2,1,0:T(8,128)}) %all-reduce.6.cloned.1.call-update) | async-done | bytes 2097168 | tf_op jit(solution)/shard_map/psum | solution.py:246
  602.0 28.6 %all-reduce.3 = (f32[256,1]{0,1:T(1,128)S(1)}, f32[256,1]{0,1:T(1,128)S(1)}) all-reduce(f32[256,1]{0,1:T(1,128)S(1)} %bitcast.99, f32[256,1]{0,1:T(1,128)S(1)} %bitcast.102), channel_id=1, replica_groups=mesh['ctx'=32,'tp'=16] {'tp'}, use_global_device_ids=true, to_apply=%region_5.6 | all-reduce | flops 512 | bytes 4096 | tf_op jit(solution)/shard_map/psum | solution.py:78
  (271 shorter events, 80.0 us)
Async XLA Ops:
  7.2 37.2 %copy-start.45 = (s32[64]{0:T(128)S(1)}, s32[64]{0:T(128)}, u32[]{:S(2)}) copy-start(s32[64]{0:T(128)} %param.33) | copy-start | bytes 772
  7.2 37.5 %copy-start.32 = (s32[64]{0:T(128)S(1)}, s32[64]{0:T(128)}, u32[]{:S(2)}) copy-start(s32[64]{0:T(128)} %param.35) | copy-start | bytes 772
  7.2 37.8 %copy-start.55 = (s32[64]{0:T(128)S(1)}, s32[64]{0:T(128)}, u32[]{:S(2)}) copy-start(s32[64]{0:T(128)} %param.34) | copy-start | bytes 772
  7.2 39.3 %copy-start.33 = (bf16[4,512]{1,0:T(4,128)(2,1)S(1)}, bf16[4,512]{1,0:T(4,128)(2,1)}, u32[]{:S(2)}) copy-start(bf16[4,512]{1,0:T(4,128)(2,1)} %param.27) | copy-start | bytes 12292
  7.2 39.3 %copy-start.44 = (bf16[4,256]{1,0:T(4,128)(2,1)S(1)}, bf16[4,256]{1,0:T(4,128)(2,1)}, u32[]{:S(2)}) copy-start(bf16[4,256]{1,0:T(4,128)(2,1)} %param.28) | copy-start | bytes 6148
  7.2 43.6 %copy-start.8 = (bf16[256,512]{1,0:T(8,128)(2,1)S(1)}, bf16[256,512]{1,0:T(8,128)(2,1)}, u32[]{:S(2)}) copy-start(bf16[256,512]{1,0:T(8,128)(2,1)} %param.23) | copy-start | bytes 786436
  7.2 588.5 %all-reduce.6.cloned.1.call-start = ((), (), s32[]{:S(2)}) async-start(), calls=%async_computation | async-start | bytes 4194304 | tf_op jit(solution)/shard_map/psum | solution.py:246
  8.3 42.5 %copy-start.27 = (bf16[16,256]{1,0:T(8,128)(2,1)S(1)}, bf16[16,256]{1,0:T(8,128)(2,1)}, u32[]{:S(2)}) copy-start(bf16[16,256]{1,0:T(8,128)(2,1)} %param.25) | copy-start | bytes 24580
  33.4 38.7 %copy-start.2 = (bf16[256,768]{1,0:T(8,128)(2,1)}, bf16[256,768]{1,0:T(8,128)(2,1)S(1)}, u32[]{:S(2)}) copy-start(bf16[256,768]{1,0:T(8,128)(2,1)S(1)} %constant_dynamic-update-slice_fusion.2) | copy-start | bytes 1179652
  33.5 38.7 %collective-permute-start.1 = (bf16[3,768]{1,0:T(4,128)(2,1)S(1)}, bf16[3,768]{1,0:T(4,128)(2,1)S(1)}, u32[]{:S(2)}, u32[]{:S(2)}) collective-permute-start(bf16[3,768]{1,0:T(4,128)(2,1)S(1)} %slice.119), channel_id=1, source_target_pairs={{0,16},{16,32},{32,48},{48,64},{64,80},{80,96},{96,112},{112,128},... | collective-permute-start | bytes 13832 | tf_op jit(solution)/shard_map/ppermute | solution.py:14
  75.0 8.8 %collective-permute-start = (f32[8,64,128]{2,1,0:T(8,128)S(1)}, f32[8,64,128]{2,1,0:T(8,128)S(1)}, u32[]{:S(2)}, u32[]{:S(2)}) collective-permute-start(f32[8,64,128]{2,1,0:T(8,128)S(1)} %multiply_add_fusion.4), channel_id=1, source_target_pairs={{0,16},{16,32},{32,48},{48,64},{64,80},{80,96},{96,112},{112,128},... | collective-permute-start | bytes 786440 | tf_op jit(solution)/shard_map/while/body/eval_jaxpr/ppermute | solution.py:14
  84.4 8.7 %collective-permute-start = (f32[8,64,128]{2,1,0:T(8,128)S(1)}, f32[8,64,128]{2,1,0:T(8,128)S(1)}, u32[]{:S(2)}, u32[]{:S(2)}) collective-permute-start(f32[8,64,128]{2,1,0:T(8,128)S(1)} %multiply_add_fusion.4), channel_id=1, source_target_pairs={{0,16},{16,32},{32,48},{48,64},{64,80},{80,96},{96,112},{112,128},... | collective-permute-start | bytes 786440 | tf_op jit(solution)/shard_map/while/body/eval_jaxpr/ppermute | solution.py:14
  93.9 7.8 %collective-permute-start = (f32[8,64,128]{2,1,0:T(8,128)S(1)}, f32[8,64,128]{2,1,0:T(8,128)S(1)}, u32[]{:S(2)}, u32[]{:S(2)}) collective-permute-start(f32[8,64,128]{2,1,0:T(8,128)S(1)} %multiply_add_fusion.4), channel_id=1, source_target_pairs={{0,16},{16,32},{32,48},{48,64},{64,80},{80,96},{96,112},{112,128},... | collective-permute-start | bytes 786440 | tf_op jit(solution)/shard_map/while/body/eval_jaxpr/ppermute | solution.py:14
  102.4 7.4 %collective-permute-start = (f32[8,64,128]{2,1,0:T(8,128)S(1)}, f32[8,64,128]{2,1,0:T(8,128)S(1)}, u32[]{:S(2)}, u32[]{:S(2)}) collective-permute-start(f32[8,64,128]{2,1,0:T(8,128)S(1)} %multiply_add_fusion.4), channel_id=1, source_target_pairs={{0,16},{16,32},{32,48},{48,64},{64,80},{80,96},{96,112},{112,128},... | collective-permute-start | bytes 786440 | tf_op jit(solution)/shard_map/while/body/eval_jaxpr/ppermute | solution.py:14
  110.5 7.1 %collective-permute-start = (f32[8,64,128]{2,1,0:T(8,128)S(1)}, f32[8,64,128]{2,1,0:T(8,128)S(1)}, u32[]{:S(2)}, u32[]{:S(2)}) collective-permute-start(f32[8,64,128]{2,1,0:T(8,128)S(1)} %multiply_add_fusion.4), channel_id=1, source_target_pairs={{0,16},{16,32},{32,48},{48,64},{64,80},{80,96},{96,112},{112,128},... | collective-permute-start | bytes 786440 | tf_op jit(solution)/shard_map/while/body/eval_jaxpr/ppermute | solution.py:14
  118.3 7.7 %collective-permute-start = (f32[8,64,128]{2,1,0:T(8,128)S(1)}, f32[8,64,128]{2,1,0:T(8,128)S(1)}, u32[]{:S(2)}, u32[]{:S(2)}) collective-permute-start(f32[8,64,128]{2,1,0:T(8,128)S(1)} %multiply_add_fusion.4), channel_id=1, source_target_pairs={{0,16},{16,32},{32,48},{48,64},{64,80},{80,96},{96,112},{112,128},... | collective-permute-start | bytes 786440 | tf_op jit(solution)/shard_map/while/body/eval_jaxpr/ppermute | solution.py:14
  126.8 8.6 %collective-permute-start = (f32[8,64,128]{2,1,0:T(8,128)S(1)}, f32[8,64,128]{2,1,0:T(8,128)S(1)}, u32[]{:S(2)}, u32[]{:S(2)}) collective-permute-start(f32[8,64,128]{2,1,0:T(8,128)S(1)} %multiply_add_fusion.4), channel_id=1, source_target_pairs={{0,16},{16,32},{32,48},{48,64},{64,80},{80,96},{96,112},{112,128},... | collective-permute-start | bytes 786440 | tf_op jit(solution)/shard_map/while/body/eval_jaxpr/ppermute | solution.py:14
  136.1 8.3 %collective-permute-start = (f32[8,64,128]{2,1,0:T(8,128)S(1)}, f32[8,64,128]{2,1,0:T(8,128)S(1)}, u32[]{:S(2)}, u32[]{:S(2)}) collective-permute-start(f32[8,64,128]{2,1,0:T(8,128)S(1)} %multiply_add_fusion.4), channel_id=1, source_target_pairs={{0,16},{16,32},{32,48},{48,64},{64,80},{80,96},{96,112},{112,128},... | collective-permute-start | bytes 786440 | tf_op jit(solution)/shard_map/while/body/eval_jaxpr/ppermute | solution.py:14
  145.1 9.1 %collective-permute-start = (f32[8,64,128]{2,1,0:T(8,128)S(1)}, f32[8,64,128]{2,1,0:T(8,128)S(1)}, u32[]{:S(2)}, u32[]{:S(2)}) collective-permute-start(f32[8,64,128]{2,1,0:T(8,128)S(1)} %multiply_add_fusion.4), channel_id=1, source_target_pairs={{0,16},{16,32},{32,48},{48,64},{64,80},{80,96},{96,112},{112,128},... | collective-permute-start | bytes 786440 | tf_op jit(solution)/shard_map/while/body/eval_jaxpr/ppermute | solution.py:14
  154.9 10.5 %collective-permute-start = (f32[8,64,128]{2,1,0:T(8,128)S(1)}, f32[8,64,128]{2,1,0:T(8,128)S(1)}, u32[]{:S(2)}, u32[]{:S(2)}) collective-permute-start(f32[8,64,128]{2,1,0:T(8,128)S(1)} %multiply_add_fusion.4), channel_id=1, source_target_pairs={{0,16},{16,32},{32,48},{48,64},{64,80},{80,96},{96,112},{112,128},... | collective-permute-start | bytes 786440 | tf_op jit(solution)/shard_map/while/body/eval_jaxpr/ppermute | solution.py:14
  166.1 11.9 %collective-permute-start = (f32[8,64,128]{2,1,0:T(8,128)S(1)}, f32[8,64,128]{2,1,0:T(8,128)S(1)}, u32[]{:S(2)}, u32[]{:S(2)}) collective-permute-start(f32[8,64,128]{2,1,0:T(8,128)S(1)} %multiply_add_fusion.4), channel_id=1, source_target_pairs={{0,16},{16,32},{32,48},{48,64},{64,80},{80,96},{96,112},{112,128},... | collective-permute-start | bytes 786440 | tf_op jit(solution)/shard_map/while/body/eval_jaxpr/ppermute | solution.py:14
  178.7 10.1 %collective-permute-start = (f32[8,64,128]{2,1,0:T(8,128)S(1)}, f32[8,64,128]{2,1,0:T(8,128)S(1)}, u32[]{:S(2)}, u32[]{:S(2)}) collective-permute-start(f32[8,64,128]{2,1,0:T(8,128)S(1)} %multiply_add_fusion.4), channel_id=1, source_target_pairs={{0,16},{16,32},{32,48},{48,64},{64,80},{80,96},{96,112},{112,128},... | collective-permute-start | bytes 786440 | tf_op jit(solution)/shard_map/while/body/eval_jaxpr/ppermute | solution.py:14
  189.5 8.8 %collective-permute-start = (f32[8,64,128]{2,1,0:T(8,128)S(1)}, f32[8,64,128]{2,1,0:T(8,128)S(1)}, u32[]{:S(2)}, u32[]{:S(2)}) collective-permute-start(f32[8,64,128]{2,1,0:T(8,128)S(1)} %multiply_add_fusion.4), channel_id=1, source_target_pairs={{0,16},{16,32},{32,48},{48,64},{64,80},{80,96},{96,112},{112,128},... | collective-permute-start | bytes 786440 | tf_op jit(solution)/shard_map/while/body/eval_jaxpr/ppermute | solution.py:14
  199.0 7.5 %collective-permute-start = (f32[8,64,128]{2,1,0:T(8,128)S(1)}, f32[8,64,128]{2,1,0:T(8,128)S(1)}, u32[]{:S(2)}, u32[]{:S(2)}) collective-permute-start(f32[8,64,128]{2,1,0:T(8,128)S(1)} %multiply_add_fusion.4), channel_id=1, source_target_pairs={{0,16},{16,32},{32,48},{48,64},{64,80},{80,96},{96,112},{112,128},... | collective-permute-start | bytes 786440 | tf_op jit(solution)/shard_map/while/body/eval_jaxpr/ppermute | solution.py:14
  207.2 8.6 %collective-permute-start = (f32[8,64,128]{2,1,0:T(8,128)S(1)}, f32[8,64,128]{2,1,0:T(8,128)S(1)}, u32[]{:S(2)}, u32[]{:S(2)}) collective-permute-start(f32[8,64,128]{2,1,0:T(8,128)S(1)} %multiply_add_fusion.4), channel_id=1, source_target_pairs={{0,16},{16,32},{32,48},{48,64},{64,80},{80,96},{96,112},{112,128},... | collective-permute-start | bytes 786440 | tf_op jit(solution)/shard_map/while/body/eval_jaxpr/ppermute | solution.py:14
  216.5 8.6 %collective-permute-start = (f32[8,64,128]{2,1,0:T(8,128)S(1)}, f32[8,64,128]{2,1,0:T(8,128)S(1)}, u32[]{:S(2)}, u32[]{:S(2)}) collective-permute-start(f32[8,64,128]{2,1,0:T(8,128)S(1)} %multiply_add_fusion.4), channel_id=1, source_target_pairs={{0,16},{16,32},{32,48},{48,64},{64,80},{80,96},{96,112},{112,128},... | collective-permute-start | bytes 786440 | tf_op jit(solution)/shard_map/while/body/eval_jaxpr/ppermute | solution.py:14
  225.8 8.8 %collective-permute-start = (f32[8,64,128]{2,1,0:T(8,128)S(1)}, f32[8,64,128]{2,1,0:T(8,128)S(1)}, u32[]{:S(2)}, u32[]{:S(2)}) collective-permute-start(f32[8,64,128]{2,1,0:T(8,128)S(1)} %multiply_add_fusion.4), channel_id=1, source_target_pairs={{0,16},{16,32},{32,48},{48,64},{64,80},{80,96},{96,112},{112,128},... | collective-permute-start | bytes 786440 | tf_op jit(solution)/shard_map/while/body/eval_jaxpr/ppermute | solution.py:14
  235.3 8.3 %collective-permute-start = (f32[8,64,128]{2,1,0:T(8,128)S(1)}, f32[8,64,128]{2,1,0:T(8,128)S(1)}, u32[]{:S(2)}, u32[]{:S(2)}) collective-permute-start(f32[8,64,128]{2,1,0:T(8,128)S(1)} %multiply_add_fusion.4), channel_id=1, source_target_pairs={{0,16},{16,32},{32,48},{48,64},{64,80},{80,96},{96,112},{112,128},... | collective-permute-start | bytes 786440 | tf_op jit(solution)/shard_map/while/body/eval_jaxpr/ppermute | solution.py:14
  244.3 9.4 %collective-permute-start = (f32[8,64,128]{2,1,0:T(8,128)S(1)}, f32[8,64,128]{2,1,0:T(8,128)S(1)}, u32[]{:S(2)}, u32[]{:S(2)}) collective-permute-start(f32[8,64,128]{2,1,0:T(8,128)S(1)} %multiply_add_fusion.4), channel_id=1, source_target_pairs={{0,16},{16,32},{32,48},{48,64},{64,80},{80,96},{96,112},{112,128},... | collective-permute-start | bytes 786440 | tf_op jit(solution)/shard_map/while/body/eval_jaxpr/ppermute | solution.py:14
  254.5 10.4 %collective-permute-start = (f32[8,64,128]{2,1,0:T(8,128)S(1)}, f32[8,64,128]{2,1,0:T(8,128)S(1)}, u32[]{:S(2)}, u32[]{:S(2)}) collective-permute-start(f32[8,64,128]{2,1,0:T(8,128)S(1)} %multiply_add_fusion.4), channel_id=1, source_target_pairs={{0,16},{16,32},{32,48},{48,64},{64,80},{80,96},{96,112},{112,128},... | collective-permute-start | bytes 786440 | tf_op jit(solution)/shard_map/while/body/eval_jaxpr/ppermute | solution.py:14
  265.5 10.0 %collective-permute-start = (f32[8,64,128]{2,1,0:T(8,128)S(1)}, f32[8,64,128]{2,1,0:T(8,128)S(1)}, u32[]{:S(2)}, u32[]{:S(2)}) collective-permute-start(f32[8,64,128]{2,1,0:T(8,128)S(1)} %multiply_add_fusion.4), channel_id=1, source_target_pairs={{0,16},{16,32},{32,48},{48,64},{64,80},{80,96},{96,112},{112,128},... | collective-permute-start | bytes 786440 | tf_op jit(solution)/shard_map/while/body/eval_jaxpr/ppermute | solution.py:14
  276.2 9.8 %collective-permute-start = (f32[8,64,128]{2,1,0:T(8,128)S(1)}, f32[8,64,128]{2,1,0:T(8,128)S(1)}, u32[]{:S(2)}, u32[]{:S(2)}) collective-permute-start(f32[8,64,128]{2,1,0:T(8,128)S(1)} %multiply_add_fusion.4), channel_id=1, source_target_pairs={{0,16},{16,32},{32,48},{48,64},{64,80},{80,96},{96,112},{112,128},... | collective-permute-start | bytes 786440 | tf_op jit(solution)/shard_map/while/body/eval_jaxpr/ppermute | solution.py:14
  286.7 11.0 %collective-permute-start = (f32[8,64,128]{2,1,0:T(8,128)S(1)}, f32[8,64,128]{2,1,0:T(8,128)S(1)}, u32[]{:S(2)}, u32[]{:S(2)}) collective-permute-start(f32[8,64,128]{2,1,0:T(8,128)S(1)} %multiply_add_fusion.4), channel_id=1, source_target_pairs={{0,16},{16,32},{32,48},{48,64},{64,80},{80,96},{96,112},{112,128},... | collective-permute-start | bytes 786440 | tf_op jit(solution)/shard_map/while/body/eval_jaxpr/ppermute | solution.py:14
  298.4 11.9 %collective-permute-start = (f32[8,64,128]{2,1,0:T(8,128)S(1)}, f32[8,64,128]{2,1,0:T(8,128)S(1)}, u32[]{:S(2)}, u32[]{:S(2)}) collective-permute-start(f32[8,64,128]{2,1,0:T(8,128)S(1)} %multiply_add_fusion.4), channel_id=1, source_target_pairs={{0,16},{16,32},{32,48},{48,64},{64,80},{80,96},{96,112},{112,128},... | collective-permute-start | bytes 786440 | tf_op jit(solution)/shard_map/while/body/eval_jaxpr/ppermute | solution.py:14
  311.0 9.8 %collective-permute-start = (f32[8,64,128]{2,1,0:T(8,128)S(1)}, f32[8,64,128]{2,1,0:T(8,128)S(1)}, u32[]{:S(2)}, u32[]{:S(2)}) collective-permute-start(f32[8,64,128]{2,1,0:T(8,128)S(1)} %multiply_add_fusion.4), channel_id=1, source_target_pairs={{0,16},{16,32},{32,48},{48,64},{64,80},{80,96},{96,112},{112,128},... | collective-permute-start | bytes 786440 | tf_op jit(solution)/shard_map/while/body/eval_jaxpr/ppermute | solution.py:14
  321.5 10.1 %collective-permute-start = (f32[8,64,128]{2,1,0:T(8,128)S(1)}, f32[8,64,128]{2,1,0:T(8,128)S(1)}, u32[]{:S(2)}, u32[]{:S(2)}) collective-permute-start(f32[8,64,128]{2,1,0:T(8,128)S(1)} %multiply_add_fusion.4), channel_id=1, source_target_pairs={{0,16},{16,32},{32,48},{48,64},{64,80},{80,96},{96,112},{112,128},... | collective-permute-start | bytes 786440 | tf_op jit(solution)/shard_map/while/body/eval_jaxpr/ppermute | solution.py:14
  332.3 8.2 %collective-permute-start = (f32[8,64,128]{2,1,0:T(8,128)S(1)}, f32[8,64,128]{2,1,0:T(8,128)S(1)}, u32[]{:S(2)}, u32[]{:S(2)}) collective-permute-start(f32[8,64,128]{2,1,0:T(8,128)S(1)} %multiply_add_fusion.4), channel_id=1, source_target_pairs={{0,16},{16,32},{32,48},{48,64},{64,80},{80,96},{96,112},{112,128},... | collective-permute-start | bytes 786440 | tf_op jit(solution)/shard_map/while/body/eval_jaxpr/ppermute | solution.py:14
  341.3 8.6 %collective-permute-start = (f32[8,64,128]{2,1,0:T(8,128)S(1)}, f32[8,64,128]{2,1,0:T(8,128)S(1)}, u32[]{:S(2)}, u32[]{:S(2)}) collective-permute-start(f32[8,64,128]{2,1,0:T(8,128)S(1)} %multiply_add_fusion.4), channel_id=1, source_target_pairs={{0,16},{16,32},{32,48},{48,64},{64,80},{80,96},{96,112},{112,128},... | collective-permute-start | bytes 786440 | tf_op jit(solution)/shard_map/while/body/eval_jaxpr/ppermute | solution.py:14
  350.6 8.3 %collective-permute-start = (f32[8,64,128]{2,1,0:T(8,128)S(1)}, f32[8,64,128]{2,1,0:T(8,128)S(1)}, u32[]{:S(2)}, u32[]{:S(2)}) collective-permute-start(f32[8,64,128]{2,1,0:T(8,128)S(1)} %multiply_add_fusion.4), channel_id=1, source_target_pairs={{0,16},{16,32},{32,48},{48,64},{64,80},{80,96},{96,112},{112,128},... | collective-permute-start | bytes 786440 | tf_op jit(solution)/shard_map/while/body/eval_jaxpr/ppermute | solution.py:14
  359.6 9.4 %collective-permute-start = (f32[8,64,128]{2,1,0:T(8,128)S(1)}, f32[8,64,128]{2,1,0:T(8,128)S(1)}, u32[]{:S(2)}, u32[]{:S(2)}) collective-permute-start(f32[8,64,128]{2,1,0:T(8,128)S(1)} %multiply_add_fusion.4), channel_id=1, source_target_pairs={{0,16},{16,32},{32,48},{48,64},{64,80},{80,96},{96,112},{112,128},... | collective-permute-start | bytes 786440 | tf_op jit(solution)/shard_map/while/body/eval_jaxpr/ppermute | solution.py:14
  369.7 10.0 %collective-permute-start = (f32[8,64,128]{2,1,0:T(8,128)S(1)}, f32[8,64,128]{2,1,0:T(8,128)S(1)}, u32[]{:S(2)}, u32[]{:S(2)}) collective-permute-start(f32[8,64,128]{2,1,0:T(8,128)S(1)} %multiply_add_fusion.4), channel_id=1, source_target_pairs={{0,16},{16,32},{32,48},{48,64},{64,80},{80,96},{96,112},{112,128},... | collective-permute-start | bytes 786440 | tf_op jit(solution)/shard_map/while/body/eval_jaxpr/ppermute | solution.py:14
  383.7 131.9 %copy-start.14 = (f32[768]{0:T(1024)S(1)}, f32[768]{0:T(1024)}, u32[]{:S(2)}) copy-start(f32[768]{0:T(1024)} %copy-done.13) | copy-start | bytes 9220
  383.7 131.9 %copy-start.19 = (s32[256]{0:T(256)S(1)}, s32[256]{0:T(256)}, u32[]{:S(2)}) copy-start(s32[256]{0:T(256)} %copy-done.18) | copy-start | bytes 3076
  383.7 131.9 %copy-start.35 = (s32[256]{0:T(256)S(1)}, s32[256]{0:T(256)}, u32[]{:S(2)}) copy-start(s32[256]{0:T(256)} %get-tuple-element.66) | copy-start | bytes 3076
  383.8 131.9 %copy-start.36 = (s32[6]{0:T(128)S(1)}, s32[6]{0:T(128)}, u32[]{:S(2)}) copy-start(s32[6]{0:T(128)} %get-tuple-element.73) | copy-start | bytes 76
  383.8 131.9 %copy-start.37 = (s32[6]{0:T(128)S(1)}, s32[6]{0:T(128)}, u32[]{:S(2)}) copy-start(s32[6]{0:T(128)} %get-tuple-element.74) | copy-start | bytes 76
  383.8 131.9 %copy-start.38 = (pred[6]{0:T(512)(128)(4,1)S(1)}, pred[6]{0:T(512)(128)(4,1)}, u32[]{:S(2)}) copy-start(pred[6]{0:T(512)(128)(4,1)} %broadcast_in_dim.287) | copy-start | bytes 22
  383.8 131.9 %copy-start.41 = (pred[256]{0:T(512)(128)(4,1)S(1)}, pred[256]{0:T(512)(128)(4,1)}, u32[]{:S(2)}) copy-start(pred[256]{0:T(512)(128)(4,1)} %get-tuple-element.61) | copy-start | bytes 772
  383.8 131.9 %copy-start.42 = (pred[256]{0:T(512)(128)(4,1)S(1)}, pred[256]{0:T(512)(128)(4,1)}, u32[]{:S(2)}) copy-start(pred[256]{0:T(512)(128)(4,1)} %get-tuple-element.62) | copy-start | bytes 772
  384.6 131.6 %copy-start.12 = (f32[768]{0:T(1024)S(1)}, f32[768]{0:T(1024)}, u32[]{:S(2)}) copy-start(f32[768]{0:T(1024)} %copy-done.11) | copy-start | bytes 9220
  384.6 131.6 %copy-start.34 = (s32[256]{0:T(256)S(1)}, s32[256]{0:T(256)}, u32[]{:S(2)}) copy-start(s32[256]{0:T(256)} %get-tuple-element.65) | copy-start | bytes 3076
  384.6 131.6 %copy-start.39 = (pred[256]{0:T(512)(128)(4,1)S(1)}, pred[256]{0:T(512)(128)(4,1)}, u32[]{:S(2)}) copy-start(pred[256]{0:T(512)(128)(4,1)} %get-tuple-element.59) | copy-start | bytes 772
  384.6 131.6 %copy-start.40 = (pred[256]{0:T(512)(128)(4,1)S(1)}, pred[256]{0:T(512)(128)(4,1)}, u32[]{:S(2)}) copy-start(pred[256]{0:T(512)(128)(4,1)} %get-tuple-element.60) | copy-start | bytes 772
  384.6 132.0 %copy-start.21 = (f32[768]{0:T(1024)S(1)}, f32[768]{0:T(1024)}, u32[]{:S(2)}) copy-start(f32[768]{0:T(1024)} %copy-done.20) | copy-start | bytes 9220
  384.6 132.0 %copy-start.23 = (f32[768]{0:T(1024)S(1)}, f32[768]{0:T(1024)}, u32[]{:S(2)}) copy-start(f32[768]{0:T(1024)} %copy-done.22) | copy-start | bytes 9220
  384.6 132.0 %copy-start.47 = (s32[256]{0:T(256)S(1)}, s32[256]{0:T(256)}, u32[]{:S(2)}) copy-start(s32[256]{0:T(256)} %get-tuple-element.64) | copy-start | bytes 3076
  384.7 132.0 %copy-start.52 = (pred[256]{0:T(512)(128)(4,1)S(1)}, pred[256]{0:T(512)(128)(4,1)}, u32[]{:S(2)}) copy-start(pred[256]{0:T(512)(128)(4,1)} %get-tuple-element.57) | copy-start | bytes 772
  384.7 132.0 %copy-start.53 = (pred[256]{0:T(512)(128)(4,1)S(1)}, pred[256]{0:T(512)(128)(4,1)}, u32[]{:S(2)}) copy-start(pred[256]{0:T(512)(128)(4,1)} %get-tuple-element.58) | copy-start | bytes 772
  518.2 79.9 %copy-start.49 = (pred[2]{0:T(512)(128)(4,1)S(1)}, pred[2]{0:T(512)(128)(4,1)}, u32[]{:S(2)}) copy-start(pred[2]{0:T(512)(128)(4,1)} %copy-done.48) | copy-start | bytes 10
  518.2 80.0 %copy-start.50 = (pred[256]{0:T(512)(128)(4,1)S(1)}, pred[256]{0:T(512)(128)(4,1)}, u32[]{:S(2)}) copy-start(pred[256]{0:T(512)(128)(4,1)} %broadcast_compare_fusion.2) | copy-start | bytes 772
  519.3 80.1 %copy-start.43 = (pred[256]{0:T(512)(128)(4,1)S(1)}, pred[256]{0:T(512)(128)(4,1)}, u32[]{:S(2)}) copy-start(pred[256]{0:T(512)(128)(4,1)} %get-tuple-element.45) | copy-start | bytes 772
  519.6 81.1 %copy-start.10 = (pred[256,256]{1,0:T(8,128)(4,1)S(1)}, pred[256,256]{1,0:T(8,128)(4,1)}, u32[]{:S(2)}) copy-start(pred[256,256]{1,0:T(8,128)(4,1)} %and_and_fusion) | copy-start | bytes 196612
  519.6 81.1 %copy-start.17 = (f32[8,256]{1,0:T(8,128)S(1)}, f32[8,256]{1,0:T(8,128)}, u32[]{:S(2)}) copy-start(f32[8,256]{1,0:T(8,128)} %copy-done.16) | copy-start | bytes 24580
  519.6 81.1 %copy-start.28 = (f32[8,256]{1,0:T(8,128)S(1)}, f32[8,256]{1,0:T(8,128)}, u32[]{:S(2)}) copy-start(f32[8,256]{1,0:T(8,128)} %copy.135) | copy-start | bytes 24580
  (27 other events, 315.9 us)
Sparse Core Ops, SparseCore 0:
  382.3 213.4 all-reduce.5
where the time goes:
time: 641 us; the launch traced here: 639 us
  waiting for transfers between devices  200 us (31%)
  blocking collectives  198 us (31%)
  starting transfers between devices  161 us (25%)
  other arithmetic  38.4 us (6%)
  local copies, waits for them, and re-layouts  16.2 us (3%)
  between operations  15.2 us (2%)
  matrix products  9.01 us (1%)
    ppermute x32, starting transfers between devices, passed_along(): lax.ppermute(value, axis, [(source, source + steps) for source in range(f...  161 us
    psum x1, blocking collectives, body(): all_states, all_tails = lax.psum((candidate, tail_rows), 'ctx')  130 us
    ppermute x32, waiting for transfers between devices, passed_along(): lax.ppermute(value, axis, [(source, source + steps) for source in range(f...  125 us
    psum x1, waiting for transfers between devices, body(): all_states, all_tails = lax.psum((candidate, tail_rows), 'ctx')  75.1 us
    psum x1, blocking collectives, finish(): total_squares = lax.psum(partial_squares, 'tp')  28.6 us
    all_gather x1, blocking collectives, body(): lax.all_gather(prefix_bc, 'tp', axis=0, tiled=True)  25.1 us
    add x31, other arithmetic, carry_step(): return passed_along(end_decay[:, None, None] * state + end_state, 'ctx', 1)  21.6 us
    all_gather x1, blocking collectives, body(): lax.all_gather(branch_bc, 'tp', axis=0, tiled=True)  14.8 us
  transfers between devices with their start and end apart: 33, of which 32 were waited for; matrix products, arithmetic and copies ran while one was open for 4% of the time, Pallas kernels for 0%

commit v1 on v0

--- a/solution.py
+++ b/solution.py
@@ -75,7 +75,18 @@
     mixed_out = mixed_out + skip[None, :, None] * values.astype(jnp.float32)
     gated = mixed_out.reshape(length, -1) * jax.nn.silu(gate_rows.astype(jnp.float32))
     partial_squares = jnp.sum(gated * gated, axis=1, keepdims=True)
-    total_squares = lax.psum(partial_squares, "tp")
+
+    def read_slabs(vector):
+        wide_n = lax.axis_size("tp")
+        opened = lambda u1: [(jj, jj ^ u1) for jj in range(wide_n)]
+        after = vector
+        for u in range(wide_n.bit_length() - 1):
+            h_now = opened(1 << u)
+            response = lax.ppermute(after, "tp", h_now)
+            after = after + response
+        return after
+
+    total_squares = read_slabs(partial_squares)
     factor = lax.rsqrt(total_squares / NORM_GROUP + EPSILON)
     return (gated * factor * gain[None, :]).astype(jnp.bfloat16)
 

time: 641 us -> 645 us (level)
  starting transfers between devices: 161 us -> 226 us
  waiting for transfers between devices: 200 us -> 167 us
  blocking collectives: 198 us -> 172 us
    ppermute x0 -> x8, starting transfers between devices: none -> 64.2 us  [read_slabs(): response = lax.ppermute(after, 'tp', h_now)]
    psum x1, waiting for transfers between devices: 75.1 us -> 37.4 us  [body(): all_states, all_tails = lax.psum((candidate, tail_rows), 'ctx')]
    psum x1 -> x0, blocking collectives: 28.6 us -> none  [finish(): total_squares = lax.psum(partial_squares, 'tp')]
  transfers between devices with their start and end apart: 33 -> 41, of which waited for: 32 -> 34; matrix products, arithmetic and copies ran while one was open for 4% -> 5% of each run, Pallas kernels for 0% -> 0%
where the time goes in v1:
time: 645 us; the launch traced here: 642 us
  starting transfers between devices  226 us (35%)
  blocking collectives  172 us (27%)
  waiting for transfers between devices  167 us (26%)
  other arithmetic  37.4 us (6%)
  local copies, waits for them, and re-layouts  15.8 us (2%)
  between operations  15.4 us (2%)
  matrix products  7.34 us (1%)
    ppermute x32, starting transfers between devices, passed_along(): lax.ppermute(value, axis, [(source, source + steps) for source in range(f...  162 us
    psum x1, blocking collectives, body(): all_states, all_tails = lax.psum((candidate, tail_rows), 'ctx')  132 us
    ppermute x32, waiting for transfers between devices, passed_along(): lax.ppermute(value, axis, [(source, source + steps) for source in range(f...  125 us
    ppermute x8, starting transfers between devices, read_slabs(): response = lax.ppermute(after, 'tp', h_now)  64.2 us
    psum x1, waiting for transfers between devices, body(): all_states, all_tails = lax.psum((candidate, tail_rows), 'ctx')  37.4 us
    all_gather x1, blocking collectives, body(): lax.all_gather(prefix_bc, 'tp', axis=0, tiled=True)  25.1 us
    add x31, other arithmetic, carry_step(): return passed_along(end_decay[:, None, None] * state + end_state, 'ctx', 1)  20.6 us
    all_gather x1, blocking collectives, body(): lax.all_gather(branch_bc, 'tp', axis=0, tiled=True)  14.8 us
  transfers between devices with their start and end apart: 41, of which 34 were waited for; matrix products, arithmetic and copies ran while one was open for 5% of the time, Pallas kernels for 0%

profile of v1, /device:TPU:1, one launch (start us, length us, event | category | flops | bytes accessed | tf_op | source)
XLA Modules:
  0.0 641.7 jit_solution(8109557423259447271)
XLA Ops:
  8.3 25.1 %all_gather.6 = bf16[256,256]{1,0:T(8,128)(2,1)S(1)} all-gather(bf16[16,256]{1,0:T(8,128)(2,1)} %param.21), channel_id=1, replica_groups=mesh['ctx'=32,'tp'=16] {'tp'}, dimensions={0}, use_global_device_ids=true | all-gather | bytes 139264 | tf_op jit(solution)/shard_map/all_gather | solution.py:208
  50.8 14.8 %all_gather.7 = bf16[256,256]{1,0:T(8,128)(2,1)S(1)} all-gather(bf16[16,256]{1,0:T(8,128)(2,1)S(1)} %copy-done.28), channel_id=1, replica_groups=mesh['ctx'=32,'tp'=16] {'tp'}, dimensions={0}, use_global_device_ids=true | all-gather | bytes 139264 | tf_op jit(solution)/shard_map/all_gather | solution.py:209
  74.3 304.6 %while.10 = (s32[]{:T(128)}, f32[8,64,128]{2,1,0:T(8,128)S(1)}, f32[8]{0:T(128)}, f32[8,64,128]{2,1,0:T(8,128)S(1)}, s32[]{:T(128)}) while((s32[]{:T(128)}, f32[8,64,128]{2,1,0:T(8,128)S(1)}, f32[8]{0:T(128)}, f32[8,64,128]{2,1,0:T(8,128)S(1)}, s32[]{:T(128)}) %tuple.49), condition=%wide.region_3.4_spmd, body=%wide.region_2.3_spmd.sunk | while | flops 131074 | bytes 1835141 | solution.py:236
  78.3 5.5 collective-permute-done
  84.4 4.1 collective-permute-start
  88.6 4.6 collective-permute-done
  93.8 4.1 collective-permute-start
  98.0 3.7 collective-permute-done
  102.3 4.1 collective-permute-start
  110.4 3.8 collective-permute-start
  114.2 3.3 collective-permute-done
  118.2 4.4 collective-permute-start
  122.6 3.3 collective-permute-done
  126.6 5.3 collective-permute-start
  131.9 3.3 collective-permute-done
  135.9 5.0 collective-permute-start
  140.9 3.3 collective-permute-done
  144.9 5.0 collective-permute-start
  149.9 4.1 collective-permute-done
  154.6 5.5 collective-permute-start
  160.1 5.1 collective-permute-done
  165.9 5.9 collective-permute-start
  171.8 5.9 collective-permute-done
  178.4 5.4 collective-permute-start
  183.8 4.7 collective-permute-done
  189.2 5.0 collective-permute-start
  194.2 3.6 collective-permute-done
  198.5 4.5 collective-permute-start
  203.0 3.3 collective-permute-done
  206.9 5.3 collective-permute-start
  216.2 5.3 collective-permute-start
  225.5 5.5 collective-permute-start
  234.9 5.0 collective-permute-start
  243.9 5.2 collective-permute-start
  249.2 4.3 collective-permute-done
  254.1 5.5 collective-permute-start
  259.6 5.2 collective-permute-done
  265.5 4.2 collective-permute-start
  269.7 6.1 collective-permute-done
  276.5 4.0 collective-permute-start
  280.5 5.3 collective-permute-done
  286.5 4.9 collective-permute-start
  291.4 5.2 collective-permute-done
  297.2 7.4 %collective-permute-start = (f32[8,64,128]{2,1,0:T(8,128)S(1)}, f32[8,64,128]{2,1,0:T(8,128)S(1)}, u32[]{:S(2)}, u32[]{:S(2)}) collective-permute-start(f32[8,64,128]{2,1,0:T(8,128)S(1)} %multiply_add_fusion.4), channel_id=1, source_target_pairs={{0,16},{16,32},{32,48},{48,64},{64,80},{80,96},{96,112},{112,128},... | collective-permute-start | bytes 786440 | tf_op jit(solution)/shard_map/while/body/eval_jaxpr/ppermute | solution.py:14
  304.7 4.9 collective-permute-done
  310.3 6.4 %collective-permute-start = (f32[8,64,128]{2,1,0:T(8,128)S(1)}, f32[8,64,128]{2,1,0:T(8,128)S(1)}, u32[]{:S(2)}, u32[]{:S(2)}) collective-permute-start(f32[8,64,128]{2,1,0:T(8,128)S(1)} %multiply_add_fusion.4), channel_id=1, source_target_pairs={{0,16},{16,32},{32,48},{48,64},{64,80},{80,96},{96,112},{112,128},... | collective-permute-start | bytes 786440 | tf_op jit(solution)/shard_map/while/body/eval_jaxpr/ppermute | solution.py:14
  316.7 3.8 collective-permute-done
  321.2 5.9 collective-permute-start
  331.0 5.3 collective-permute-start
  340.3 5.8 collective-permute-start
  350.1 5.0 collective-permute-start
  359.1 5.9 collective-permute-start
  368.9 6.2 collective-permute-start
  375.2 3.8 collective-permute-done
  384.4 33.6 %collective-permute-start.2 = (f32[256,1]{0,1:T(1,128)S(1)}, f32[256,1]{0,1:T(1,128)S(1)}, u32[]{:S(2)}, u32[]{:S(2)}) collective-permute-start(f32[256,1]{0,1:T(1,128)S(1)} %bitcast.99), channel_id=1, source_target_pairs={{0,1},{1,0},{2,3},{3,2},{4,5},{5,4},{6,7},{7,6},{8,9},{9,8},{10,11... | collective-permute-start | bytes 3080 | tf_op jit(solution)/shard_map/ppermute | solution.py:85
  418.3 132.1 %psum.14 = bf16[8,3,768]{2,1,0:T(4,128)(2,1)S(1)} all-reduce(f32[8,3,768]{2,1,0:T(4,128)S(1)} %reshape.508), channel_id=1, replica_groups=mesh['ctx'=32,'tp'=16] {'ctx'}, use_global_device_ids=true, to_apply=%region_13.14 | all-reduce | flops 18432 | bytes 110592 | tf_op jit(solution)/shard_map/psum | solution.py:257
  553.8 3.6 collective-permute-start.3
  557.4 37.4 %all-reduce.5.cloned.1.call-done = f32[8,8,64,128]{3,2,1,0:T(8,128)} async-done(((f32[8,8,64,128]{3,2,1,0:T(8,128)}), f32[8,8,64,128]{3,2,1,0:T(8,128)}) %all-reduce.5.cloned.1.call-update) | async-done | bytes 2097168 | tf_op jit(solution)/shard_map/psum | solution.py:257
  601.0 6.5 %collective-permute-start.6 = (f32[256,1]{0,1:T(1,128)S(1)}, f32[256,1]{0,1:T(1,128)S(1)}, u32[]{:S(2)}, u32[]{:S(2)}) collective-permute-start(f32[256,1]{0,1:T(1,128)S(1)} %bitcast.101), channel_id=1, source_target_pairs={{0,1},{1,0},{2,3},{3,2},{4,5},{5,4},{6,7},{7,6},{8,9},{9,8},{10,11... | collective-permute-start | bytes 3080 | tf_op jit(solution)/shard_map/ppermute | solution.py:85
  607.5 4.3 collective-permute-start.4
  611.9 3.3 collective-permute-start.7
  615.2 5.2 collective-permute-start.5
  620.5 3.4 collective-permute-start.8
  625.7 4.2 collective-permute-start.9
  (294 shorter events, 104.7 us)
Async XLA Ops:
  7.2 587.5 %all-reduce.5.cloned.1.call-start = ((), (), s32[]{:S(2)}) async-start(), calls=%async_computation | async-start | bytes 4194304 | tf_op jit(solution)/shard_map/psum | solution.py:257
  33.5 38.8 %collective-permute-start.1 = (bf16[3,768]{1,0:T(4,128)(2,1)S(1)}, bf16[3,768]{1,0:T(4,128)(2,1)S(1)}, u32[]{:S(2)}, u32[]{:S(2)}) collective-permute-start(bf16[3,768]{1,0:T(4,128)(2,1)S(1)} %slice.119), channel_id=1, source_target_pairs={{0,16},{16,32},{32,48},{48,64},{64,80},{80,96},{96,112},{112,128},... | collective-permute-start | bytes 13832 | tf_op jit(solution)/shard_map/ppermute | solution.py:14
  75.0 8.7 %collective-permute-start = (f32[8,64,128]{2,1,0:T(8,128)S(1)}, f32[8,64,128]{2,1,0:T(8,128)S(1)}, u32[]{:S(2)}, u32[]{:S(2)}) collective-permute-start(f32[8,64,128]{2,1,0:T(8,128)S(1)} %multiply_add_fusion.4), channel_id=1, source_target_pairs={{0,16},{16,32},{32,48},{48,64},{64,80},{80,96},{96,112},{112,128},... | collective-permute-start | bytes 786440 | tf_op jit(solution)/shard_map/while/body/eval_jaxpr/ppermute | solution.py:14
  84.4 8.7 %collective-permute-start = (f32[8,64,128]{2,1,0:T(8,128)S(1)}, f32[8,64,128]{2,1,0:T(8,128)S(1)}, u32[]{:S(2)}, u32[]{:S(2)}) collective-permute-start(f32[8,64,128]{2,1,0:T(8,128)S(1)} %multiply_add_fusion.4), channel_id=1, source_target_pairs={{0,16},{16,32},{32,48},{48,64},{64,80},{80,96},{96,112},{112,128},... | collective-permute-start | bytes 786440 | tf_op jit(solution)/shard_map/while/body/eval_jaxpr/ppermute | solution.py:14
  93.8 7.8 %collective-permute-start = (f32[8,64,128]{2,1,0:T(8,128)S(1)}, f32[8,64,128]{2,1,0:T(8,128)S(1)}, u32[]{:S(2)}, u32[]{:S(2)}) collective-permute-start(f32[8,64,128]{2,1,0:T(8,128)S(1)} %multiply_add_fusion.4), channel_id=1, source_target_pairs={{0,16},{16,32},{32,48},{48,64},{64,80},{80,96},{96,112},{112,128},... | collective-permute-start | bytes 786440 | tf_op jit(solution)/shard_map/while/body/eval_jaxpr/ppermute | solution.py:14
  102.3 7.4 %collective-permute-start = (f32[8,64,128]{2,1,0:T(8,128)S(1)}, f32[8,64,128]{2,1,0:T(8,128)S(1)}, u32[]{:S(2)}, u32[]{:S(2)}) collective-permute-start(f32[8,64,128]{2,1,0:T(8,128)S(1)} %multiply_add_fusion.4), channel_id=1, source_target_pairs={{0,16},{16,32},{32,48},{48,64},{64,80},{80,96},{96,112},{112,128},... | collective-permute-start | bytes 786440 | tf_op jit(solution)/shard_map/while/body/eval_jaxpr/ppermute | solution.py:14
  110.4 7.1 %collective-permute-start = (f32[8,64,128]{2,1,0:T(8,128)S(1)}, f32[8,64,128]{2,1,0:T(8,128)S(1)}, u32[]{:S(2)}, u32[]{:S(2)}) collective-permute-start(f32[8,64,128]{2,1,0:T(8,128)S(1)} %multiply_add_fusion.4), channel_id=1, source_target_pairs={{0,16},{16,32},{32,48},{48,64},{64,80},{80,96},{96,112},{112,128},... | collective-permute-start | bytes 786440 | tf_op jit(solution)/shard_map/while/body/eval_jaxpr/ppermute | solution.py:14
  118.2 7.7 %collective-permute-start = (f32[8,64,128]{2,1,0:T(8,128)S(1)}, f32[8,64,128]{2,1,0:T(8,128)S(1)}, u32[]{:S(2)}, u32[]{:S(2)}) collective-permute-start(f32[8,64,128]{2,1,0:T(8,128)S(1)} %multiply_add_fusion.4), channel_id=1, source_target_pairs={{0,16},{16,32},{32,48},{48,64},{64,80},{80,96},{96,112},{112,128},... | collective-permute-start | bytes 786440 | tf_op jit(solution)/shard_map/while/body/eval_jaxpr/ppermute | solution.py:14
  126.6 8.6 %collective-permute-start = (f32[8,64,128]{2,1,0:T(8,128)S(1)}, f32[8,64,128]{2,1,0:T(8,128)S(1)}, u32[]{:S(2)}, u32[]{:S(2)}) collective-permute-start(f32[8,64,128]{2,1,0:T(8,128)S(1)} %multiply_add_fusion.4), channel_id=1, source_target_pairs={{0,16},{16,32},{32,48},{48,64},{64,80},{80,96},{96,112},{112,128},... | collective-permute-start | bytes 786440 | tf_op jit(solution)/shard_map/while/body/eval_jaxpr/ppermute | solution.py:14
  135.9 8.3 %collective-permute-start = (f32[8,64,128]{2,1,0:T(8,128)S(1)}, f32[8,64,128]{2,1,0:T(8,128)S(1)}, u32[]{:S(2)}, u32[]{:S(2)}) collective-permute-start(f32[8,64,128]{2,1,0:T(8,128)S(1)} %multiply_add_fusion.4), channel_id=1, source_target_pairs={{0,16},{16,32},{32,48},{48,64},{64,80},{80,96},{96,112},{112,128},... | collective-permute-start | bytes 786440 | tf_op jit(solution)/shard_map/while/body/eval_jaxpr/ppermute | solution.py:14
  144.9 9.1 %collective-permute-start = (f32[8,64,128]{2,1,0:T(8,128)S(1)}, f32[8,64,128]{2,1,0:T(8,128)S(1)}, u32[]{:S(2)}, u32[]{:S(2)}) collective-permute-start(f32[8,64,128]{2,1,0:T(8,128)S(1)} %multiply_add_fusion.4), channel_id=1, source_target_pairs={{0,16},{16,32},{32,48},{48,64},{64,80},{80,96},{96,112},{112,128},... | collective-permute-start | bytes 786440 | tf_op jit(solution)/shard_map/while/body/eval_jaxpr/ppermute | solution.py:14
  154.6 10.6 %collective-permute-start = (f32[8,64,128]{2,1,0:T(8,128)S(1)}, f32[8,64,128]{2,1,0:T(8,128)S(1)}, u32[]{:S(2)}, u32[]{:S(2)}) collective-permute-start(f32[8,64,128]{2,1,0:T(8,128)S(1)} %multiply_add_fusion.4), channel_id=1, source_target_pairs={{0,16},{16,32},{32,48},{48,64},{64,80},{80,96},{96,112},{112,128},... | collective-permute-start | bytes 786440 | tf_op jit(solution)/shard_map/while/body/eval_jaxpr/ppermute | solution.py:14
  165.9 11.8 %collective-permute-start = (f32[8,64,128]{2,1,0:T(8,128)S(1)}, f32[8,64,128]{2,1,0:T(8,128)S(1)}, u32[]{:S(2)}, u32[]{:S(2)}) collective-permute-start(f32[8,64,128]{2,1,0:T(8,128)S(1)} %multiply_add_fusion.4), channel_id=1, source_target_pairs={{0,16},{16,32},{32,48},{48,64},{64,80},{80,96},{96,112},{112,128},... | collective-permute-start | bytes 786440 | tf_op jit(solution)/shard_map/while/body/eval_jaxpr/ppermute | solution.py:14
  178.4 10.1 %collective-permute-start = (f32[8,64,128]{2,1,0:T(8,128)S(1)}, f32[8,64,128]{2,1,0:T(8,128)S(1)}, u32[]{:S(2)}, u32[]{:S(2)}) collective-permute-start(f32[8,64,128]{2,1,0:T(8,128)S(1)} %multiply_add_fusion.4), channel_id=1, source_target_pairs={{0,16},{16,32},{32,48},{48,64},{64,80},{80,96},{96,112},{112,128},... | collective-permute-start | bytes 786440 | tf_op jit(solution)/shard_map/while/body/eval_jaxpr/ppermute | solution.py:14
  189.2 8.6 %collective-permute-start = (f32[8,64,128]{2,1,0:T(8,128)S(1)}, f32[8,64,128]{2,1,0:T(8,128)S(1)}, u32[]{:S(2)}, u32[]{:S(2)}) collective-permute-start(f32[8,64,128]{2,1,0:T(8,128)S(1)} %multiply_add_fusion.4), channel_id=1, source_target_pairs={{0,16},{16,32},{32,48},{48,64},{64,80},{80,96},{96,112},{112,128},... | collective-permute-start | bytes 786440 | tf_op jit(solution)/shard_map/while/body/eval_jaxpr/ppermute | solution.py:14
  198.5 7.8 %collective-permute-start = (f32[8,64,128]{2,1,0:T(8,128)S(1)}, f32[8,64,128]{2,1,0:T(8,128)S(1)}, u32[]{:S(2)}, u32[]{:S(2)}) collective-permute-start(f32[8,64,128]{2,1,0:T(8,128)S(1)} %multiply_add_fusion.4), channel_id=1, source_target_pairs={{0,16},{16,32},{32,48},{48,64},{64,80},{80,96},{96,112},{112,128},... | collective-permute-start | bytes 786440 | tf_op jit(solution)/shard_map/while/body/eval_jaxpr/ppermute | solution.py:14
  206.9 8.6 %collective-permute-start = (f32[8,64,128]{2,1,0:T(8,128)S(1)}, f32[8,64,128]{2,1,0:T(8,128)S(1)}, u32[]{:S(2)}, u32[]{:S(2)}) collective-permute-start(f32[8,64,128]{2,1,0:T(8,128)S(1)} %multiply_add_fusion.4), channel_id=1, source_target_pairs={{0,16},{16,32},{32,48},{48,64},{64,80},{80,96},{96,112},{112,128},... | collective-permute-start | bytes 786440 | tf_op jit(solution)/shard_map/while/body/eval_jaxpr/ppermute | solution.py:14
  216.2 8.6 %collective-permute-start = (f32[8,64,128]{2,1,0:T(8,128)S(1)}, f32[8,64,128]{2,1,0:T(8,128)S(1)}, u32[]{:S(2)}, u32[]{:S(2)}) collective-permute-start(f32[8,64,128]{2,1,0:T(8,128)S(1)} %multiply_add_fusion.4), channel_id=1, source_target_pairs={{0,16},{16,32},{32,48},{48,64},{64,80},{80,96},{96,112},{112,128},... | collective-permute-start | bytes 786440 | tf_op jit(solution)/shard_map/while/body/eval_jaxpr/ppermute | solution.py:14
  225.5 8.8 %collective-permute-start = (f32[8,64,128]{2,1,0:T(8,128)S(1)}, f32[8,64,128]{2,1,0:T(8,128)S(1)}, u32[]{:S(2)}, u32[]{:S(2)}) collective-permute-start(f32[8,64,128]{2,1,0:T(8,128)S(1)} %multiply_add_fusion.4), channel_id=1, source_target_pairs={{0,16},{16,32},{32,48},{48,64},{64,80},{80,96},{96,112},{112,128},... | collective-permute-start | bytes 786440 | tf_op jit(solution)/shard_map/while/body/eval_jaxpr/ppermute | solution.py:14
  234.9 8.3 %collective-permute-start = (f32[8,64,128]{2,1,0:T(8,128)S(1)}, f32[8,64,128]{2,1,0:T(8,128)S(1)}, u32[]{:S(2)}, u32[]{:S(2)}) collective-permute-start(f32[8,64,128]{2,1,0:T(8,128)S(1)} %multiply_add_fusion.4), channel_id=1, source_target_pairs={{0,16},{16,32},{32,48},{48,64},{64,80},{80,96},{96,112},{112,128},... | collective-permute-start | bytes 786440 | tf_op jit(solution)/shard_map/while/body/eval_jaxpr/ppermute | solution.py:14
  243.9 9.5 %collective-permute-start = (f32[8,64,128]{2,1,0:T(8,128)S(1)}, f32[8,64,128]{2,1,0:T(8,128)S(1)}, u32[]{:S(2)}, u32[]{:S(2)}) collective-permute-start(f32[8,64,128]{2,1,0:T(8,128)S(1)} %multiply_add_fusion.4), channel_id=1, source_target_pairs={{0,16},{16,32},{32,48},{48,64},{64,80},{80,96},{96,112},{112,128},... | collective-permute-start | bytes 786440 | tf_op jit(solution)/shard_map/while/body/eval_jaxpr/ppermute | solution.py:14
  254.1 10.8 %collective-permute-start = (f32[8,64,128]{2,1,0:T(8,128)S(1)}, f32[8,64,128]{2,1,0:T(8,128)S(1)}, u32[]{:S(2)}, u32[]{:S(2)}) collective-permute-start(f32[8,64,128]{2,1,0:T(8,128)S(1)} %multiply_add_fusion.4), channel_id=1, source_target_pairs={{0,16},{16,32},{32,48},{48,64},{64,80},{80,96},{96,112},{112,128},... | collective-permute-start | bytes 786440 | tf_op jit(solution)/shard_map/while/body/eval_jaxpr/ppermute | solution.py:14
  265.5 10.3 %collective-permute-start = (f32[8,64,128]{2,1,0:T(8,128)S(1)}, f32[8,64,128]{2,1,0:T(8,128)S(1)}, u32[]{:S(2)}, u32[]{:S(2)}) collective-permute-start(f32[8,64,128]{2,1,0:T(8,128)S(1)} %multiply_add_fusion.4), channel_id=1, source_target_pairs={{0,16},{16,32},{32,48},{48,64},{64,80},{80,96},{96,112},{112,128},... | collective-permute-start | bytes 786440 | tf_op jit(solution)/shard_map/while/body/eval_jaxpr/ppermute | solution.py:14
  276.5 9.3 %collective-permute-start = (f32[8,64,128]{2,1,0:T(8,128)S(1)}, f32[8,64,128]{2,1,0:T(8,128)S(1)}, u32[]{:S(2)}, u32[]{:S(2)}) collective-permute-start(f32[8,64,128]{2,1,0:T(8,128)S(1)} %multiply_add_fusion.4), channel_id=1, source_target_pairs={{0,16},{16,32},{32,48},{48,64},{64,80},{80,96},{96,112},{112,128},... | collective-permute-start | bytes 786440 | tf_op jit(solution)/shard_map/while/body/eval_jaxpr/ppermute | solution.py:14
  286.5 10.1 %collective-permute-start = (f32[8,64,128]{2,1,0:T(8,128)S(1)}, f32[8,64,128]{2,1,0:T(8,128)S(1)}, u32[]{:S(2)}, u32[]{:S(2)}) collective-permute-start(f32[8,64,128]{2,1,0:T(8,128)S(1)} %multiply_add_fusion.4), channel_id=1, source_target_pairs={{0,16},{16,32},{32,48},{48,64},{64,80},{80,96},{96,112},{112,128},... | collective-permute-start | bytes 786440 | tf_op jit(solution)/shard_map/while/body/eval_jaxpr/ppermute | solution.py:14
  297.2 12.4 %collective-permute-start = (f32[8,64,128]{2,1,0:T(8,128)S(1)}, f32[8,64,128]{2,1,0:T(8,128)S(1)}, u32[]{:S(2)}, u32[]{:S(2)}) collective-permute-start(f32[8,64,128]{2,1,0:T(8,128)S(1)} %multiply_add_fusion.4), channel_id=1, source_target_pairs={{0,16},{16,32},{32,48},{48,64},{64,80},{80,96},{96,112},{112,128},... | collective-permute-start | bytes 786440 | tf_op jit(solution)/shard_map/while/body/eval_jaxpr/ppermute | solution.py:14
  310.3 10.3 %collective-permute-start = (f32[8,64,128]{2,1,0:T(8,128)S(1)}, f32[8,64,128]{2,1,0:T(8,128)S(1)}, u32[]{:S(2)}, u32[]{:S(2)}) collective-permute-start(f32[8,64,128]{2,1,0:T(8,128)S(1)} %multiply_add_fusion.4), channel_id=1, source_target_pairs={{0,16},{16,32},{32,48},{48,64},{64,80},{80,96},{96,112},{112,128},... | collective-permute-start | bytes 786440 | tf_op jit(solution)/shard_map/while/body/eval_jaxpr/ppermute | solution.py:14
  321.2 9.1 %collective-permute-start = (f32[8,64,128]{2,1,0:T(8,128)S(1)}, f32[8,64,128]{2,1,0:T(8,128)S(1)}, u32[]{:S(2)}, u32[]{:S(2)}) collective-permute-start(f32[8,64,128]{2,1,0:T(8,128)S(1)} %multiply_add_fusion.4), channel_id=1, source_target_pairs={{0,16},{16,32},{32,48},{48,64},{64,80},{80,96},{96,112},{112,128},... | collective-permute-start | bytes 786440 | tf_op jit(solution)/shard_map/while/body/eval_jaxpr/ppermute | solution.py:14
  331.0 8.6 %collective-permute-start = (f32[8,64,128]{2,1,0:T(8,128)S(1)}, f32[8,64,128]{2,1,0:T(8,128)S(1)}, u32[]{:S(2)}, u32[]{:S(2)}) collective-permute-start(f32[8,64,128]{2,1,0:T(8,128)S(1)} %multiply_add_fusion.4), channel_id=1, source_target_pairs={{0,16},{16,32},{32,48},{48,64},{64,80},{80,96},{96,112},{112,128},... | collective-permute-start | bytes 786440 | tf_op jit(solution)/shard_map/while/body/eval_jaxpr/ppermute | solution.py:14
  340.3 9.1 %collective-permute-start = (f32[8,64,128]{2,1,0:T(8,128)S(1)}, f32[8,64,128]{2,1,0:T(8,128)S(1)}, u32[]{:S(2)}, u32[]{:S(2)}) collective-permute-start(f32[8,64,128]{2,1,0:T(8,128)S(1)} %multiply_add_fusion.4), channel_id=1, source_target_pairs={{0,16},{16,32},{32,48},{48,64},{64,80},{80,96},{96,112},{112,128},... | collective-permute-start | bytes 786440 | tf_op jit(solution)/shard_map/while/body/eval_jaxpr/ppermute | solution.py:14
  350.1 8.3 %collective-permute-start = (f32[8,64,128]{2,1,0:T(8,128)S(1)}, f32[8,64,128]{2,1,0:T(8,128)S(1)}, u32[]{:S(2)}, u32[]{:S(2)}) collective-permute-start(f32[8,64,128]{2,1,0:T(8,128)S(1)} %multiply_add_fusion.4), channel_id=1, source_target_pairs={{0,16},{16,32},{32,48},{48,64},{64,80},{80,96},{96,112},{112,128},... | collective-permute-start | bytes 786440 | tf_op jit(solution)/shard_map/while/body/eval_jaxpr/ppermute | solution.py:14
  359.1 9.2 %collective-permute-start = (f32[8,64,128]{2,1,0:T(8,128)S(1)}, f32[8,64,128]{2,1,0:T(8,128)S(1)}, u32[]{:S(2)}, u32[]{:S(2)}) collective-permute-start(f32[8,64,128]{2,1,0:T(8,128)S(1)} %multiply_add_fusion.4), channel_id=1, source_target_pairs={{0,16},{16,32},{32,48},{48,64},{64,80},{80,96},{96,112},{112,128},... | collective-permute-start | bytes 786440 | tf_op jit(solution)/shard_map/while/body/eval_jaxpr/ppermute | solution.py:14
  368.9 10.1 %collective-permute-start = (f32[8,64,128]{2,1,0:T(8,128)S(1)}, f32[8,64,128]{2,1,0:T(8,128)S(1)}, u32[]{:S(2)}, u32[]{:S(2)}) collective-permute-start(f32[8,64,128]{2,1,0:T(8,128)S(1)} %multiply_add_fusion.4), channel_id=1, source_target_pairs={{0,16},{16,32},{32,48},{48,64},{64,80},{80,96},{96,112},{112,128},... | collective-permute-start | bytes 786440 | tf_op jit(solution)/shard_map/while/body/eval_jaxpr/ppermute | solution.py:14
  383.7 167.3 %copy-start.15 = (f32[768]{0:T(1024)S(1)}, f32[768]{0:T(1024)}, u32[]{:S(2)}) copy-start(f32[768]{0:T(1024)} %copy-done.14) | copy-start | bytes 9220
  383.7 167.3 %copy-start.20 = (s32[256]{0:T(256)S(1)}, s32[256]{0:T(256)}, u32[]{:S(2)}) copy-start(s32[256]{0:T(256)} %copy-done.19) | copy-start | bytes 3076
  383.7 167.3 %copy-start.36 = (s32[256]{0:T(256)S(1)}, s32[256]{0:T(256)}, u32[]{:S(2)}) copy-start(s32[256]{0:T(256)} %get-tuple-element.64) | copy-start | bytes 3076
  383.8 167.3 %copy-start.37 = (s32[6]{0:T(128)S(1)}, s32[6]{0:T(128)}, u32[]{:S(2)}) copy-start(s32[6]{0:T(128)} %get-tuple-element.71) | copy-start | bytes 76
  383.8 167.3 %copy-start.38 = (s32[6]{0:T(128)S(1)}, s32[6]{0:T(128)}, u32[]{:S(2)}) copy-start(s32[6]{0:T(128)} %get-tuple-element.72) | copy-start | bytes 76
  383.8 167.3 %copy-start.39 = (pred[6]{0:T(512)(128)(4,1)S(1)}, pred[6]{0:T(512)(128)(4,1)}, u32[]{:S(2)}) copy-start(pred[6]{0:T(512)(128)(4,1)} %broadcast_in_dim.287) | copy-start | bytes 22
  383.8 167.3 %copy-start.42 = (pred[256]{0:T(512)(128)(4,1)S(1)}, pred[256]{0:T(512)(128)(4,1)}, u32[]{:S(2)}) copy-start(pred[256]{0:T(512)(128)(4,1)} %get-tuple-element.59) | copy-start | bytes 772
  383.8 167.3 %copy-start.43 = (pred[256]{0:T(512)(128)(4,1)S(1)}, pred[256]{0:T(512)(128)(4,1)}, u32[]{:S(2)}) copy-start(pred[256]{0:T(512)(128)(4,1)} %get-tuple-element.60) | copy-start | bytes 772
  383.8 167.7 %copy-start.13 = (f32[768]{0:T(1024)S(1)}, f32[768]{0:T(1024)}, u32[]{:S(2)}) copy-start(f32[768]{0:T(1024)} %copy-done.12) | copy-start | bytes 9220
  383.8 167.7 %copy-start.35 = (s32[256]{0:T(256)S(1)}, s32[256]{0:T(256)}, u32[]{:S(2)}) copy-start(s32[256]{0:T(256)} %get-tuple-element.63) | copy-start | bytes 3076
  383.8 167.7 %copy-start.40 = (pred[256]{0:T(512)(128)(4,1)S(1)}, pred[256]{0:T(512)(128)(4,1)}, u32[]{:S(2)}) copy-start(pred[256]{0:T(512)(128)(4,1)} %get-tuple-element.57) | copy-start | bytes 772
  383.8 167.7 %copy-start.41 = (pred[256]{0:T(512)(128)(4,1)S(1)}, pred[256]{0:T(512)(128)(4,1)}, u32[]{:S(2)}) copy-start(pred[256]{0:T(512)(128)(4,1)} %get-tuple-element.58) | copy-start | bytes 772
  384.1 168.0 %copy-start.22 = (f32[768]{0:T(1024)S(1)}, f32[768]{0:T(1024)}, u32[]{:S(2)}) copy-start(f32[768]{0:T(1024)} %copy-done.21) | copy-start | bytes 9220
  384.1 168.0 %copy-start.24 = (f32[768]{0:T(1024)S(1)}, f32[768]{0:T(1024)}, u32[]{:S(2)}) copy-start(f32[768]{0:T(1024)} %copy-done.23) | copy-start | bytes 9220
  384.1 168.0 %copy-start.48 = (s32[256]{0:T(256)S(1)}, s32[256]{0:T(256)}, u32[]{:S(2)}) copy-start(s32[256]{0:T(256)} %get-tuple-element.62) | copy-start | bytes 3076
  384.1 168.0 %copy-start.53 = (pred[256]{0:T(512)(128)(4,1)S(1)}, pred[256]{0:T(512)(128)(4,1)}, u32[]{:S(2)}) copy-start(pred[256]{0:T(512)(128)(4,1)} %get-tuple-element.55) | copy-start | bytes 772
  384.1 168.0 %copy-start.54 = (pred[256]{0:T(512)(128)(4,1)S(1)}, pred[256]{0:T(512)(128)(4,1)}, u32[]{:S(2)}) copy-start(pred[256]{0:T(512)(128)(4,1)} %get-tuple-element.56) | copy-start | bytes 772
  384.4 169.4 %collective-permute-start.2 = (f32[256,1]{0,1:T(1,128)S(1)}, f32[256,1]{0,1:T(1,128)S(1)}, u32[]{:S(2)}, u32[]{:S(2)}) collective-permute-start(f32[256,1]{0,1:T(1,128)S(1)} %bitcast.99), channel_id=1, source_target_pairs={{0,1},{1,0},{2,3},{3,2},{4,5},{5,4},{6,7},{7,6},{8,9},{9,8},{10,11... | collective-permute-start | bytes 3080 | tf_op jit(solution)/shard_map/ppermute | solution.py:85
  552.8 44.2 %copy-start.50 = (pred[2]{0:T(512)(128)(4,1)S(1)}, pred[2]{0:T(512)(128)(4,1)}, u32[]{:S(2)}) copy-start(pred[2]{0:T(512)(128)(4,1)} %copy-done.49) | copy-start | bytes 10
  552.8 44.3 %copy-start.51 = (pred[256]{0:T(512)(128)(4,1)S(1)}, pred[256]{0:T(512)(128)(4,1)}, u32[]{:S(2)}) copy-start(pred[256]{0:T(512)(128)(4,1)} %broadcast_compare_fusion.2) | copy-start | bytes 772
  553.6 44.9 %copy-start.44 = (pred[256]{0:T(512)(128)(4,1)S(1)}, pred[256]{0:T(512)(128)(4,1)}, u32[]{:S(2)}) copy-start(pred[256]{0:T(512)(128)(4,1)} %get-tuple-element.43) | copy-start | bytes 772
  553.6 46.1 %copy-start.11 = (pred[256,256]{1,0:T(8,128)(4,1)S(1)}, pred[256,256]{1,0:T(8,128)(4,1)}, u32[]{:S(2)}) copy-start(pred[256,256]{1,0:T(8,128)(4,1)} %and_and_fusion) | copy-start | bytes 196612
  553.6 46.1 %copy-start.18 = (f32[8,256]{1,0:T(8,128)S(1)}, f32[8,256]{1,0:T(8,128)}, u32[]{:S(2)}) copy-start(f32[8,256]{1,0:T(8,128)} %copy-done.17) | copy-start | bytes 24580
  553.6 46.1 %copy-start.29 = (f32[8,256]{1,0:T(8,128)S(1)}, f32[8,256]{1,0:T(8,128)}, u32[]{:S(2)}) copy-start(f32[8,256]{1,0:T(8,128)} %copy.135) | copy-start | bytes 24580
  553.8 53.7 %collective-permute-start.3 = (f32[256,1]{0,1:T(1,128)S(1)}, f32[256,1]{0,1:T(1,128)S(1)}, u32[]{:S(2)}, u32[]{:S(2)}) collective-permute-start(f32[256,1]{0,1:T(1,128)S(1)} %add.270), channel_id=1, source_target_pairs={{0,2},{1,3},{2,0},{3,1},{4,6},{5,7},{6,4},{7,5},{8,10},{9,11},{10,... | collective-permute-start | bytes 3080 | tf_op jit(solution)/shard_map/ppermute | solution.py:85
  601.0 10.9 %collective-permute-start.6 = (f32[256,1]{0,1:T(1,128)S(1)}, f32[256,1]{0,1:T(1,128)S(1)}, u32[]{:S(2)}, u32[]{:S(2)}) collective-permute-start(f32[256,1]{0,1:T(1,128)S(1)} %bitcast.101), channel_id=1, source_target_pairs={{0,1},{1,0},{2,3},{3,2},{4,5},{5,4},{6,7},{7,6},{8,9},{9,8},{10,11... | collective-permute-start | bytes 3080 | tf_op jit(solution)/shard_map/ppermute | solution.py:85
  607.5 7.7 %collective-permute-start.4 = (f32[256,1]{0,1:T(1,128)S(1)}, f32[256,1]{0,1:T(1,128)S(1)}, u32[]{:S(2)}, u32[]{:S(2)}) collective-permute-start(f32[256,1]{0,1:T(1,128)S(1)} %add.271), channel_id=1, source_target_pairs={{0,4},{1,5},{2,6},{3,7},{4,0},{5,1},{6,2},{7,3},{8,12},{9,13},{10,... | collective-permute-start | bytes 3080 | tf_op jit(solution)/shard_map/ppermute | solution.py:85
  611.9 8.6 %collective-permute-start.7 = (f32[256,1]{0,1:T(1,128)S(1)}, f32[256,1]{0,1:T(1,128)S(1)}, u32[]{:S(2)}, u32[]{:S(2)}) collective-permute-start(f32[256,1]{0,1:T(1,128)S(1)} %add.305), channel_id=1, source_target_pairs={{0,2},{1,3},{2,0},{3,1},{4,6},{5,7},{6,4},{7,5},{8,10},{9,11},{10,... | collective-permute-start | bytes 3080 | tf_op jit(solution)/shard_map/ppermute | solution.py:85
  615.2 8.7 %collective-permute-start.5 = (f32[256,1]{0,1:T(1,128)S(1)}, f32[256,1]{0,1:T(1,128)S(1)}, u32[]{:S(2)}, u32[]{:S(2)}) collective-permute-start(f32[256,1]{0,1:T(1,128)S(1)} %add.272), channel_id=1, source_target_pairs={{0,8},{1,9},{2,10},{3,11},{4,12},{5,13},{6,14},{7,15},{8,0},{9,1},... | collective-permute-start | bytes 3080 | tf_op jit(solution)/shard_map/ppermute | solution.py:85
  620.5 5.2 collective-permute-start.8
  625.7 8.2 %collective-permute-start.9 = (f32[256,1]{0,1:T(1,128)S(1)}, f32[256,1]{0,1:T(1,128)S(1)}, u32[]{:S(2)}, u32[]{:S(2)}) collective-permute-start(f32[256,1]{0,1:T(1,128)S(1)} %add.307), channel_id=1, source_target_pairs={{0,8},{1,9},{2,10},{3,11},{4,12},{5,13},{6,14},{7,15},{8,0},{9,1},... | collective-permute-start | bytes 3080 | tf_op jit(solution)/shard_map/ppermute | solution.py:85
  (36 other events, 771.0 us)
Sparse Core Ops, SparseCore 0:
  381.5 213.2 all-reduce.4
